TPU v7x, 256 devices: a whole 4x4x8 slice. The times are simulated.
256 devices in a mesh: dp: 8 (over z), space: 32 (over y, x, core).
Axes of the slice: x: 4, y: 4, z: 8, core: 2. Of those that a mesh axis runs over, the one named last changes fastest.
Arguments:
- latents: bfloat16 [8, 256, 256, 320], P('dp', 'space'), may hold values from -14 to 14
- gain_one: float32 [320], replicated, may hold values from 0.1 to 1.9
- shift_one: float32 [320], replicated, may hold values from -2.5 to 2.5
- kernel_one: bfloat16 [3, 3, 320, 320], P(None, None, None, 'dp'), may hold values from -0.109375 to 0.109375
- time_shift: float32 [8, 320], P('dp'), may hold values from -4 to 4
- gain_two: float32 [320], replicated, may hold values from 0.1 to 1.9
- shift_two: float32 [320], replicated, may hold values from -2.5 to 2.5
- kernel_two: bfloat16 [3, 3, 320, 320], P(None, None, None, 'dp'), may hold values from -0.109375 to 0.109375
- bias_two: float32 [320], replicated, may hold values from -2.5 to 2.5
Outputs:
- block_out: bfloat16 [8, 256, 256, 320], P('dp', 'space')
All inputs are finite; a program needn't handle non-finite values.
Results may differ from a plain program's by a relative error of at most 0.0041.
Values may be sent and summed in bfloat16 or wider, within the bound.
A program may use at most 128 MiB of HBM per device.

v0:
```python
import jax
import jax.numpy as jnp
from jax import lax
from jax.sharding import PartitionSpec as P

GROUPS = 32


epsilon = 1e-05


def extended(cells, sides, width):
    for axis, dim in sides:
        count = lax.axis_size(axis)
        ends = count - 1
        head = lax.slice_in_dim(cells, 0, width, axis=dim)
        tail = lax.slice_in_dim(cells, cells.shape[dim] - width, cells.shape[dim], axis=dim)
        cells = jnp.concatenate(
            [
                lax.ppermute(tail, axis, [(i, (i + 1) % count) for i in range(ends)]),
                cells,
                lax.ppermute(head, axis, [((i + 1) % count, i) for i in range(ends)]),
            ],
            axis=dim,
        )
    return cells


def normalize(values, gain, shift):
    images, rows, cols, channels = values.shape
    width_group = channels // GROUPS
    count = rows * lax.axis_size("space") * cols * width_group
    grouped = values.reshape(images, rows, cols, GROUPS, width_group)
    mean = lax.psum(jnp.sum(grouped, axis=(1, 2, 4)), "space") / count
    centered = grouped - mean[:, None, None, :, None]
    var = lax.psum(jnp.sum(centered * centered, axis=(1, 2, 4)), "space") / count
    scaled = centered * lax.rsqrt(var + epsilon)[:, None, None, :, None]
    normed = scaled.reshape(values.shape) * gain + shift
    return jax.nn.silu(normed).astype(jnp.bfloat16)


def convolve(act, kernel):
    images, rows, cols, channels = act.shape
    padded = extended(act, (("space", 1),), 1)
    padded = jnp.pad(padded, ((0, 0), (0, 0), (1, 1), (0, 0)))
    positions = images * rows * cols
    space_count = lax.axis_size("space")
    dp_count = lax.axis_size("dp")
    part_in = channels // space_count
    part_out = kernel.shape[3]
    mine = lax.dynamic_slice_in_dim(kernel, lax.axis_index("space") * part_in, part_in, 2)
    pieces = lax.all_gather(mine[None], ("dp", "space"), axis=0, tiled=True)
    full_kernel = pieces.reshape(dp_count, space_count, 3, 3, part_in, part_out)
    full_kernel = full_kernel.transpose(2, 3, 1, 4, 0, 5).reshape(
        3, 3, channels, dp_count * part_out
    )
    total = jnp.zeros((positions, full_kernel.shape[3]), jnp.float32)
    for row_tap in range(3):
        for col_tap in range(3):
            window = padded[:, row_tap : row_tap + rows, col_tap : col_tap + cols, :].reshape(
                positions, channels
            )
            total = total + jnp.dot(
                window, full_kernel[row_tap, col_tap], preferred_element_type=jnp.float32
            )
    return total.reshape(images, rows, cols, channels)


def local(
    latents, gain_one, shift_one, kernel_one, time_shift, gain_two, shift_two, kernel_two, bias_two
):
    source = latents.astype(jnp.float32)
    act_one = normalize(source, gain_one, shift_one)
    hidden = convolve(act_one, kernel_one) + time_shift[:, None, None, :]
    act_two = normalize(hidden, gain_two, shift_two)
    result = convolve(act_two, kernel_two) + bias_two + source
    return result.astype(jnp.bfloat16)


def solution(mesh):
    return jax.shard_map(
        local,
        mesh=mesh,
        in_specs=(
            P("dp", "space", None, None),
            P(),
            P(),
            P(None, None, None, "dp"),
            P("dp", None),
            P(),
            P(),
            P(None, None, None, "dp"),
            P(),
        ),
        out_specs=P("dp", "space", None, None),
        check_vma=False,
    )
```

profile of v0, /device:TPU:1, one launch (start us, length us, event | category | flops | bytes accessed | tf_op | source)
XLA Modules:
  0.0 382.8 jit_solution(12017420370805208113)
XLA Ops:
  8.4 1.6 convert_reduce_fusion
  10.2 65.3 %psum.28 = f32[1,32]{1,0:T(1,128)S(1)} all-reduce(f32[1,32]{1,0:T(1,128)S(1)} %bitcast.252), channel_id=1, replica_groups=mesh['dp'=8,'space'=32] {'space'}, use_global_device_ids=true, to_apply=%region_2.0 | all-reduce | flops 32 | bytes 256 | tf_op jit(solution)/shard_map/psum | solution.py:34
  76.5 65.8 %psum.29 = f32[1,32]{1,0:T(1,128)S(1)} all-reduce(f32[1,32]{1,0:T(1,128)S(1)} %bitcast.253), channel_id=1, replica_groups=mesh['dp'=8,'space'=32] {'space'}, use_global_device_ids=true, to_apply=%region_5.6 | all-reduce | flops 32 | bytes 256 | tf_op jit(solution)/shard_map/psum | solution.py:36
  142.4 1.3 fusion.11
  143.8 1.9 collective-permute-start
  145.7 2.9 collective-permute-start.1
  150.5 1.4 fusion.52
  153.4 1.3 copy.65
  155.9 1.6 fusion.21
  157.5 2.2 fusion.32
  159.7 1.3 copy.66
  161.2 1.3 copy.63
  162.5 1.2 copy.61
  163.8 1.3 copy.60
  166.3 10.5 %copy.111 = bf16[8,32,3,3,10,40]{5,0,4,1,3,2:T(8,128)(2,1)} copy(bf16[8,32,3,3,10,40]{5,3,4,2,1,0:T(4,128)(2,1)} %bitcast.217) | data formatting | bytes 3686400 | tf_op jit(solution)/shard_map/reshape | solution.py:53
  176.8 8.5 %reshape.221 = bf16[3,3,320,320]{3,2,1,0:T(8,128)(2,1)} reshape(bf16[3,3,32,10,8,40]{5,4,3,2,1,0:T(8,128)(2,1)} %bitcast.211) | data formatting | bytes 3686400 | tf_op jit(solution)/shard_map/reshape | solution.py:54
  185.4 2.4 fusion.29
  196.6 2.4 add_reduce_fusion
  199.2 61.6 %psum.30 = f32[1,32]{1,0:T(1,128)S(1)} all-reduce(f32[1,32]{1,0:T(1,128)S(1)} %bitcast.254), channel_id=1, replica_groups=mesh['dp'=8,'space'=32] {'space'}, use_global_device_ids=true, to_apply=%region_8.9 | all-reduce | flops 32 | bytes 256 | tf_op jit(solution)/shard_map/psum | solution.py:34
  261.0 2.3 multiply_reduce_fusion
  263.6 63.8 %psum.31 = f32[1,32]{1,0:T(1,128)S(1)} all-reduce(f32[1,32]{1,0:T(1,128)S(1)} %bitcast.251), channel_id=1, replica_groups=mesh['dp'=8,'space'=32] {'space'}, use_global_device_ids=true, to_apply=%region_11.12 | all-reduce | flops 32 | bytes 256 | tf_op jit(solution)/shard_map/psum | solution.py:36
  327.6 2.9 copy.67
  330.5 1.6 multiply_convert_fusion.1
  332.1 1.9 collective-permute-start.2
  334.1 2.6 collective-permute-start.3
  336.7 10.6 %copy.110 = bf16[8,32,3,3,10,40]{5,0,4,1,3,2:T(8,128)(2,1)} copy(bf16[8,32,3,3,10,40]{5,3,4,2,1,0:T(4,128)(2,1)} %bitcast.216) | data formatting | bytes 3686400 | tf_op jit(solution)/shard_map/reshape | solution.py:53
  347.4 8.4 %reshape.233 = bf16[3,3,320,320]{3,2,1,0:T(8,128)(2,1)} reshape(bf16[3,3,32,10,8,40]{5,4,3,2,1,0:T(8,128)(2,1)} %bitcast.212) | data formatting | bytes 3686400 | tf_op jit(solution)/shard_map/reshape | solution.py:54
  356.3 1.7 select_maximum_fusion
  358.0 2.5 fusion.31
  361.5 1.3 copy-done.5
  367.2 1.5 convolution_add_fusion.4
  373.5 2.2 fusion.12
  (105 shorter events, 29.4 us)
Async XLA Ops:
  6.5 1.0 copy-start
  6.5 69.2 %copy-start.2 = (bf16[1,8,256,320]{2,3,1,0:T(8,128)(2,1)S(1)}, bf16[1,8,256,320]{2,3,1,0:T(8,128)(2,1)}, u32[]{:S(2)}) copy-start(bf16[1,8,256,320]{2,3,1,0:T(8,128)(2,1)} %param.9) | copy-start | bytes 3932164
  6.5 135.9 %copy-start.13 = (f32[320]{0:T(512)S(1)}, f32[320]{0:T(512)}, u32[]{:S(2)}) copy-start(f32[320]{0:T(512)} %param.11) | copy-start | bytes 3844
  6.5 135.9 %copy-start.14 = (f32[320]{0:T(512)S(1)}, f32[320]{0:T(512)}, u32[]{:S(2)}) copy-start(f32[320]{0:T(512)} %param.10) | copy-start | bytes 3844
  6.5 159.7 %all-gather.5.cloned.1.call-start = ((), (), s32[]{:S(2)}) async-start(), calls=%async_computation | async-start | bytes 7895040 | tf_op jit(solution)/shard_map/all_gather | solution.py:52
  8.4 328.3 %all-gather.7.cloned.1.call-start = ((), (), s32[]{:S(2)}) async-start(), calls=%async_computation.1 | async-start | bytes 7895040 | tf_op jit(solution)/shard_map/all_gather | solution.py:52
  143.8 9.3 %collective-permute-start = (bf16[1,1,256,320]{2,3,1,0:T(8,128)(2,1)S(1)}, bf16[1,1,256,320]{2,3,1,0:T(8,128)(2,1)S(1)}, u32[]{:S(2)}, u32[]{:S(2)}) collective-permute-start(bf16[1,1,256,320]{2,3,1,0:T(8,128)(2,1)S(1)} %get-tuple-element.23), channel_id=1, source_target_pairs={{0,1},{1,2},{2,3},{3,4},{4,5},{5,6},{6,7},{7,8},{8,9},{9,10},{10,1... | collective-permute-start | bytes 491528 | tf_op jit(solution)/shard_map/ppermute | solution.py:20
  145.7 7.4 %collective-permute-start.1 = (bf16[1,1,256,320]{2,3,1,0:T(8,128)(2,1)S(1)}, bf16[1,1,256,320]{2,3,1,0:T(8,128)(2,1)S(1)}, u32[]{:S(2)}, u32[]{:S(2)}) collective-permute-start(bf16[1,1,256,320]{2,3,1,0:T(8,128)(2,1)S(1)} %get-tuple-element.24), channel_id=1, source_target_pairs={{1,0},{2,1},{3,2},{4,3},{5,4},{6,5},{7,6},{8,7},{9,8},{10,9},{11,1... | collective-permute-start | bytes 491528 | tf_op jit(solution)/shard_map/ppermute | solution.py:22
  150.5 2.6 copy-start.18
  185.4 2.4 copy-start.4
  185.4 2.4 copy-start.8
  187.8 1.3 copy-start.11
  189.1 1.3 copy-start.10
  190.5 1.3 copy-start.6
  191.8 1.3 copy-start.9
  194.0 1.3 copy-start.7
  195.3 1.3 copy-start.12
  327.5 2.9 copy-start.15
  327.6 2.9 copy-start.16
  332.1 23.6 %collective-permute-start.2 = (bf16[1,1,256,320]{2,3,1,0:T(8,128)(2,1)S(1)}, bf16[1,1,256,320]{2,3,1,0:T(8,128)(2,1)S(1)}, u32[]{:S(2)}, u32[]{:S(2)}) collective-permute-start(bf16[1,1,256,320]{2,3,1,0:T(8,128)(2,1)S(1)} %get-tuple-element.19), channel_id=1, source_target_pairs={{0,1},{1,2},{2,3},{3,4},{4,5},{5,6},{6,7},{7,8},{8,9},{9,10},{10,1... | collective-permute-start | bytes 491528 | tf_op jit(solution)/shard_map/ppermute | solution.py:20
  334.1 21.7 %collective-permute-start.3 = (bf16[1,1,256,320]{2,3,1,0:T(8,128)(2,1)S(1)}, bf16[1,1,256,320]{2,3,1,0:T(8,128)(2,1)S(1)}, u32[]{:S(2)}, u32[]{:S(2)}) collective-permute-start(bf16[1,1,256,320]{2,3,1,0:T(8,128)(2,1)S(1)} %get-tuple-element.20), channel_id=1, source_target_pairs={{1,0},{2,1},{3,2},{4,3},{5,4},{6,5},{7,6},{8,7},{9,8},{10,9},{11,1... | collective-permute-start | bytes 491528 | tf_op jit(solution)/shard_map/ppermute | solution.py:22
  361.1 1.6 copy-start.5
  365.5 1.7 copy-start.3
  372.3 1.2 copy-start.17
  373.5 2.2 copy-start.1
Sparse Core Ops, SparseCore 0:
  11.0 121.6 all-gather.4
  150.6 116.1 all-gather.6
where the time goes:
time: 387 us; the launch traced here: 383 us
  blocking collectives  256 us (66%)
  local copies, waits for them, and re-layouts  67.8 us (18%)
  matrix products  19.6 us (5%)
  other arithmetic  15.1 us (4%)
  between operations  14.2 us (4%)
  starting transfers between devices  9.48 us (2%)
    psum x2, blocking collectives, normalize(): lax.psum(jnp.sum(centered * centered, axis=(1, 2, 4)), 'space') / count  130 us
    psum x2, blocking collectives, normalize(): mean = lax.psum(jnp.sum(grouped, axis=(1, 2, 4)), 'space') / count  127 us
    unnamed x59, local copies, waits for them, and re-layouts  22.7 us
    reshape x2, local copies, waits for them, and re-layouts, convolve(): full_kernel = pieces.reshape(dp_count, space_count, 3, 3, part_in, part_out)  21.2 us
    dot_general x18, matrix products, convolve(): jnp.dot(window, full_kernel[row_tap, col_tap], preferred_element_type=jnp...  19.6 us
    reshape x2, local copies, waits for them, and re-layouts, convolve(): full_kernel.transpose(2, 3, 1, 4, 0, 5)  17 us
  transfers between devices with their start and end apart: 6, of which 0 were waited for; matrix products, arithmetic and copies ran while one was open for 20% of the time, Pallas kernels for 0%

commit v1 on v0

v1 whole, which is shorter than its diff:
```python
import functools

import jax
import jax.numpy as jnp
from jax import lax
from jax.experimental import pallas as pl
from jax.experimental.pallas import tpu as pltpu
from jax.sharding import PartitionSpec as P

MESH = pl.DeviceIdType.MESH
BF = jnp.bfloat16
F32 = jnp.float32
C = 320
MAIN = 256
LEFT = 64
TILES = 8
EPSILON = 1e-05
NZ = 8
NS = 32
ROWS = 8
COLS = 256
ORDER = (1, 7, 2, 6, 3, 5, 4)


def group_matrix():
    rows = lax.broadcasted_iota(jnp.int32, (384, 384), 0)
    cols = lax.broadcasted_iota(jnp.int32, (384, 384), 1)
    same = ((rows * 6554) >> 16) == ((cols * 6554) >> 16)
    return jnp.where(same, 1.0, 0.0).astype(BF)


def group_sum(vec, gmat):
    hi = vec.astype(BF)
    rest = vec - hi.astype(F32)
    mid = rest.astype(BF)
    low = (rest - mid.astype(F32)).astype(BF)
    lhs = jnp.concatenate([hi, mid, low, jnp.zeros((13, 384), BF)], axis=0)
    out = jnp.dot(lhs, gmat, preferred_element_type=F32)
    return out[0:1] + out[1:2] + out[2:3]


def to_lanes(block):
    return jnp.concatenate([block[0:1], block[1:2], block[2:3]], axis=1)


def to_rows(vec):
    return jnp.concatenate([vec[:, 0:128], vec[:, 128:256], vec[:, 256:384]], axis=0)


def combine(recv, gmat):
    means = recv[:, 0:3, :]
    squares = jnp.sum(recv[:, 3:6, :], axis=0)
    mean = group_sum(to_lanes(jnp.sum(means, axis=0)), gmat) * (1.0 / (NS * 10))
    centered = means - to_rows(mean)[None]
    total = squares + float(ROWS * COLS) * jnp.sum(centered * centered, axis=0)
    var = group_sum(to_lanes(total), gmat) * (1.0 / (10 * NS * ROWS * COLS))
    return mean[:, :C], lax.rsqrt(var + EPSILON)[:, :C]


def put_stats(st_ref, mean, squares):
    st_ref[...] = jnp.zeros((8, 128), F32)
    for first, vec in ((0, mean), (3, squares)):
        st_ref[first : first + 1, :] = vec[:, 0:128]
        st_ref[first + 1 : first + 2, :] = vec[:, 128:256]
        st_ref[first + 2 : first + 3, 0:64] = vec[:, 256:320]


def silu(v):
    half = 0.5 * v
    return half + half * jnp.tanh(half)


def spread(act):
    zero = jnp.zeros((1, C), BF)
    before = jnp.concatenate([zero, act[: COLS - 1]], axis=0)
    after = jnp.concatenate([act[1:], zero], axis=0)
    rest = jnp.concatenate(
        [before[:, MAIN:], act[:, MAIN:], after[:, MAIN:], jnp.zeros((COLS, LEFT), BF)], axis=1
    )
    return before[:, :MAIN], act[:, :MAIN], after[:, :MAIN], rest


def put_spread(a3, row, act):
    for i, part in enumerate(spread(act)):
        a3[row, :, i * 256 : (i + 1) * 256] = part


def kernel(
    lat, g1, b1, k1, ts, g2, b2, k2, bias, out,
    x, a3, hm, hl, hid, kv, gath, wm, wl, gmat, st, recv, hs, hr, ob,
    lsem, osem, hsem, hrsem, ssem, srsem, wsem, wrsem,
):
    z = lax.axis_index("dp")
    s = lax.axis_index("space")
    y, xx, c = s // 8, (s // 2) % 4, s % 2
    part = c * 4 + (y % 2) * 2 + xx % 2

    barrier = pltpu.get_barrier_semaphore()
    for d in range(1, NS):
        pl.semaphore_signal(barrier, inc=1, device_id=(z, (s + d) % NS), device_id_type=MESH)
    for d in range(1, NZ):
        pl.semaphore_signal(barrier, inc=1, device_id=((z + d) % NZ, s), device_id_type=MESH)

    load_x = pltpu.make_async_copy(lat.at[0], x.at[pl.ds(1, ROWS)], lsem.at[0])
    load_k = [pltpu.make_async_copy(k, kv.at[i], lsem.at[1 + i]) for i, k in enumerate((k1, k2))]
    load_k[0].start()
    load_x.start()
    load_k[1].start()
    gmat[...] = group_matrix()

    def remote(src, dst, send, got, device):
        return pltpu.make_async_remote_copy(
            src_ref=src, dst_ref=dst, send_sem=send, recv_sem=got, device_id=device, device_id_type=MESH
        )

    def pack(n):
        for dy in range(3):
            taps = [kv[n, dy, dx].astype(F32).T for dx in range(3)]
            flat = jnp.concatenate(
                [t[:, :MAIN] for t in taps] + [t[:, MAIN:] for t in taps] + [jnp.zeros((40, LEFT), F32)],
                axis=1,
            ).astype(BF)
            for p in range(TILES):
                gath[n, p, z, dy * 40 : dy * 40 + 40, :] = flat[:, p * 128 : (p + 1) * 128]
        for p in range(TILES):
            gath[n, p, z, 120:128, :] = jnp.zeros((8, 128), BF)

    def first(n, d):
        block = gath.at[n, part, z]
        return remote(block, block, wsem.at[n, d], wrsem.at[n, d], ((z + d) % NZ, s))

    def plane(y_step, x_step):
        return ((y + y_step) % 4 * 4 + (xx + x_step) % 4) * 2 + c

    def second(n, d):
        block = gath.at[n, part, (z - d) % NZ]
        sx = 1 if d % 2 == 0 else 3
        sy = 1 if (d // 2) % 2 == 0 else 3
        targets = (plane(0, sx), plane(sx, 0), plane(sy, sx))
        return [
            remote(block, block, wsem.at[n, 8 * (i + 1) + d], wrsem.at[n, 8 * (i + 1) + d], (z, t))
            for i, t in enumerate(targets)
        ]

    def third(n, d):
        block = gath.at[n, pl.ds(c * 4, 4), (z - d) % NZ]
        other = s + 1 - 2 * c
        return remote(block, block, wsem.at[n, 32 + d], wrsem.at[n, 32 + d], (z, other))

    def start_first(n):
        for d in ORDER:
            first(n, d).start()

    def go_second(n, d):
        first(n, d).wait_recv()
        for copy in second(n, d):
            copy.start()

    def go_third(n, d):
        for copy in second(n, d):
            copy.wait_recv()
        third(n, d).start()

    def end_gather(n):
        for d in ORDER:
            third(n, d).wait_recv()

    def drain(n):
        for d in ORDER:
            first(n, d).wait_send()
            for copy in second(n, d):
                copy.wait_send()
            third(n, d).wait_send()

    def arrange(n):
        for o in range(NZ):
            for dy in range(3):
                low = o * 40
                for p in range(TILES):
                    seg = gath[n, p, o, dy * 40 : dy * 40 + 40, :]
                    cols = slice(dy * 1024 + p * 128, dy * 1024 + p * 128 + 128)
                    side = slice(p * 128, p * 128 + 128)
                    if low + 40 <= MAIN:
                        wm[n, low : low + 40, cols] = seg
                    elif low >= MAIN:
                        at = dy * LEFT + low - MAIN
                        wl[n, at : at + 40, side] = seg
                    else:
                        cut = MAIN - low
                        wm[n, low:MAIN, cols] = seg[:cut]
                        wl[n, dy * LEFT : dy * LEFT + 40 - cut, side] = seg[cut:]

    def stat_copy(n, d):
        return remote(st.at[n], recv.at[n, d - 1], ssem.at[n, d], srsem.at[n], (z, (s + d) % NS))

    def send_stats(n):
        for d in range(1, NS):
            stat_copy(n, d).start()
        recv[n, NS - 1] = st[n]

    def wait_stats(n):
        pltpu.make_async_copy(recv.at[n, pl.ds(0, NS - 1)], recv.at[n, pl.ds(0, NS - 1)], srsem.at[n]).wait()

    def nt(a, b):
        return lax.dot_general(a, b, (((1,), (1,)), ((), ())), preferred_element_type=F32)

    def conv_main(n, row, rows):
        lhs = jnp.concatenate([a3[row + d : row + d + rows].reshape(rows * COLS, 1024) for d in range(3)], axis=1)
        hm[row : row + rows] = nt(lhs, wm[n]).reshape(rows, COLS, MAIN)

    def conv_left(n, row, rows):
        hl[row : row + rows] = nt(a3[row : row + rows].reshape(rows * COLS, 1024), wl[n]).reshape(
            rows, COLS, 3 * LEFT
        )

    def conv_row(row):
        side = hl[row, :, 0:64] + hl[row + 1, :, 64:128] + hl[row + 2, :, 128:192]
        return jnp.concatenate([hm[row], side], axis=1)

    load_k[0].wait()
    pack(0)
    load_x.wait()

    def sum_row(i, total):
        return total + jnp.sum(x[1 + i].astype(F32), axis=0, keepdims=True)

    mean = lax.fori_loop(0, ROWS, sum_row, jnp.zeros((1, C), F32)) * (1.0 / (ROWS * COLS))

    def square_row(i, total):
        v = x[1 + i].astype(F32) - mean
        return total + jnp.sum(v * v, axis=0, keepdims=True)

    squares = lax.fori_loop(0, ROWS, square_row, jnp.zeros((1, C), F32))
    put_stats(st.at[0], mean, squares)

    pl.semaphore_wait(barrier, NS - 1 + NZ - 1)
    start_first(0)
    send_stats(0)
    halo = [
        remote(x.at[1], x.at[9], hsem.at[0], hrsem.at[0], (z, (s + NS - 1) % NS)),
        remote(x.at[8], x.at[0], hsem.at[1], hrsem.at[1], (z, (s + 1) % NS)),
    ]
    for copy in halo:
        copy.start()
    load_k[1].wait()
    pack(1)
    go_second(0, 1)
    go_second(0, 7)
    go_second(0, 2)
    go_second(0, 6)
    wait_stats(0)
    mean, inv = combine(recv[0], gmat[...])
    scale, offset = inv * g1[...].reshape(1, C), b1[...].reshape(1, C)

    def act_row(i, carry):
        put_spread(a3, i, silu((x[i].astype(F32) - mean) * scale + offset).astype(BF))
        return carry

    lax.fori_loop(1, 1 + ROWS, act_row, 0)
    go_second(0, 3)
    go_second(0, 5)
    go_third(0, 1)
    go_third(0, 7)
    go_second(0, 4)
    start_first(1)
    go_third(0, 2)
    go_third(0, 6)

    def halo_act(values, edge):
        return jnp.where(s == edge, 0.0, silu((values.astype(F32) - mean) * scale + offset)).astype(BF)

    for copy in halo:
        copy.wait_recv()
    put_spread(a3, 0, halo_act(x[0], 0))
    put_spread(a3, 9, halo_act(x[9], NS - 1))
    go_third(0, 3)
    go_third(0, 5)
    go_third(0, 4)
    end_gather(0)
    arrange(0)

    conv_main(0, 0, 4)
    go_second(1, 1)
    go_second(1, 7)
    conv_main(0, 4, 4)
    for d in ORDER[2:]:
        go_second(1, d)
    conv_left(0, 0, 10)
    shift = ts[...]

    def hidden_sum(i, total):
        side = hl[i, :, 0:64] + hl[i + 1, :, 64:128] + hl[i + 2, :, 128:192]
        v = jnp.concatenate([hm[i], side], axis=1) + shift
        hid[i] = v
        return total + jnp.sum(v, axis=0, keepdims=True)

    mean = lax.fori_loop(0, ROWS, hidden_sum, jnp.zeros((1, C), F32)) * (1.0 / (ROWS * COLS))

    def hidden_square(i, total):
        v = hid[i] - mean
        return total + jnp.sum(v * v, axis=0, keepdims=True)

    squares = lax.fori_loop(0, ROWS, hidden_square, jnp.zeros((1, C), F32))
    put_stats(st.at[1], mean, squares)
    send_stats(1)
    for d in ORDER:
        go_third(1, d)
    end_gather(1)
    arrange(1)
    wait_stats(1)
    mean2, inv2 = combine(recv[1], gmat[...])
    scale2, offset2 = inv2 * g2[...].reshape(1, C), b2[...].reshape(1, C)

    def act_two(i):
        return silu((hid[i] - mean2) * scale2 + offset2).astype(BF)

    sides = []
    for i, (row, step) in enumerate(((0, NS - 1), (ROWS - 1, 1))):
        act = act_two(row)
        hs[i] = act
        copy = remote(hs.at[i], hr.at[1 - i], hsem.at[2 + i], hrsem.at[2 + i], (z, (s + step) % NS))
        copy.start()
        sides.append(copy)
        put_spread(a3, 1 + row, act)

    def act_two_row(i, carry):
        put_spread(a3, 1 + i, act_two(i))
        return carry

    lax.fori_loop(1, ROWS - 1, act_two_row, 0)
    conv_main(1, 1, 6)
    conv_left(1, 1, 8)
    for copy in sides:
        copy.wait_recv()
    zero = jnp.zeros((COLS, C), BF)
    put_spread(a3, 0, jnp.where(s == 0, zero, hr[0]))
    put_spread(a3, 9, jnp.where(s == NS - 1, zero, hr[1]))
    conv_main(1, 0, 1)
    conv_main(1, 7, 1)
    conv_left(1, 0, 1)
    conv_left(1, 9, 1)
    last = bias[...].reshape(1, C)

    def out_row(i, carry):
        side = hl[i, :, 0:64] + hl[i + 1, :, 64:128] + hl[i + 2, :, 128:192]
        v = jnp.concatenate([hm[i], side], axis=1) + last + x[1 + i].astype(F32)
        ob[i] = v.astype(BF)
        return carry

    lax.fori_loop(0, ROWS, out_row, 0)
    store = pltpu.make_async_copy(ob, out.at[0], osem)
    store.start()
    for n in range(2):
        for d in range(1, NS):
            stat_copy(n, d).wait_send()
        drain(n)
    for copy in halo + sides:
        copy.wait_send()
    store.wait()


def local(latents, gain_one, shift_one, kernel_one, time_shift, gain_two, shift_two, kernel_two, bias_two):
    hbm = pl.BlockSpec(memory_space=pl.ANY)
    vmem = pl.BlockSpec(memory_space=pltpu.VMEM)
    return pl.pallas_call(
        kernel,
        out_shape=jax.ShapeDtypeStruct((1, ROWS, COLS, C), BF),
        in_specs=[hbm, vmem, vmem, hbm, vmem, vmem, vmem, hbm, vmem],
        out_specs=hbm,
        scratch_shapes=[
            pltpu.VMEM((10, COLS, C), BF),
            pltpu.VMEM((10, COLS, 1024), BF),
            pltpu.VMEM((ROWS, COLS, MAIN), F32),
            pltpu.VMEM((10, COLS, 3 * LEFT), F32),
            pltpu.VMEM((ROWS, COLS, C), F32),
            pltpu.VMEM((2, 3, 3, C, 40), BF),
            pltpu.VMEM((2, TILES, NZ, 128, 128), BF),
            pltpu.VMEM((2, MAIN, 3072), BF),
            pltpu.VMEM((2, 3 * LEFT, 1024), BF),
            pltpu.VMEM((384, 384), BF),
            pltpu.VMEM((2, 8, 128), F32),
            pltpu.VMEM((2, NS, 8, 128), F32),
            pltpu.VMEM((2, COLS, C), BF),
            pltpu.VMEM((2, COLS, C), BF),
            pltpu.VMEM((ROWS, COLS, C), BF),
            pltpu.SemaphoreType.DMA((3,)),
            pltpu.SemaphoreType.DMA,
            pltpu.SemaphoreType.DMA((4,)),
            pltpu.SemaphoreType.DMA((4,)),
            pltpu.SemaphoreType.DMA((2, NS)),
            pltpu.SemaphoreType.DMA((2,)),
            pltpu.SemaphoreType.DMA((2, 40)),
            pltpu.SemaphoreType.DMA((2, 40)),
        ],
        compiler_params=pltpu.CompilerParams(
            collective_id=0, has_side_effects=True, vmem_limit_bytes=60 * 2**20
        ),
        name="block",
    )(latents, gain_one, shift_one, kernel_one, time_shift, gain_two, shift_two, kernel_two, bias_two)


def solution(mesh):
    return jax.shard_map(
        local,
        mesh=mesh,
        in_specs=(
            P("dp", "space", None, None),
            P(),
            P(),
            P(None, None, None, "dp"),
            P("dp", None),
            P(),
            P(),
            P(None, None, None, "dp"),
            P(),
        ),
        out_specs=P("dp", "space", None, None),
        check_vma=False,
    )
```

time: 387 us -> 63.9 us (0.17); the launches traced: 383 us -> 63.7 us
  blocking collectives: 256 us -> 0 us
  local copies, waits for them, and re-layouts: 67.8 us -> 8.42 us
  Pallas kernels: 0 us -> 55.3 us
  matrix products: 19.6 us -> 0 us
  other arithmetic: 15.1 us -> 0 us
  between operations: 14.2 us -> 0.01 us
  starting transfers between devices: 9.48 us -> 0 us
    psum x4 -> x0, blocking collectives: 256 us -> none  [the longest x2 130 us: normalize(): lax.psum(jnp.sum(centered * centered, axis=(1, 2, 4)), 'space') / count]
    pallas_call x0 -> x1, Pallas kernels: none -> 55.3 us  [local(): pl.pallas_call(kernel, out_shape=jax.ShapeDtypeStruct((1, ROWS, COLS, C),...]
    reshape x4 -> x0, local copies, waits for them, and re-layouts: 38.1 us -> none  [the longest x2 21.2 us: convolve(): full_kernel = pieces.reshape(dp_count, space_count, 3, 3, part_in, part_out)]
    dot_general x18 -> x0, matrix products: 19.6 us -> none  [convolve(): jnp.dot(window, full_kernel[row_tap, col_tap], preferred_element_type=jnp...]
    unnamed x59 -> x5, local copies, waits for them, and re-layouts: 22.7 us -> 5.88 us
    ppermute x4 -> x0, starting transfers between devices: 9.4 us -> none  [the longest x2 5.56 us: extended(): lax.ppermute(head, axis, [((i + 1) % count, i) for i in range(ends)])]
    convert_element_type x3 -> x0, other arithmetic: 5.1 us -> none  [the longest x2 2.95 us: normalize(): return jax.nn.silu(normed).astype(jnp.bfloat16)]
    reduce_sum x7 -> x0, other arithmetic: 4.86 us -> none  [the longest x4 3.04 us: normalize(): jnp.sum(centered * centered, axis=(1, 2, 4))]
  transfers between devices with their start and end apart: 6 -> 0, of which waited for: 0 -> 0; matrix products, arithmetic and copies ran while one was open for 20% -> 0% of each run, Pallas kernels for 0% -> 0%
where the time goes in v1:
time: 63.9 us; the launch traced here: 63.7 us
  Pallas kernels  55.3 us (87%)
  local copies, waits for them, and re-layouts  8.42 us (13%)
    pallas_call x1, Pallas kernels, local(): pl.pallas_call(kernel, out_shape=jax.ShapeDtypeStruct((1, ROWS, COLS, C),...  55.3 us
    unnamed x5, local copies, waits for them, and re-layouts  5.88 us
    pallas_call x1, local copies, waits for them, and re-layouts, local(): pl.pallas_call(kernel, out_shape=jax.ShapeDtypeStruct((1, ROWS, COLS, C),...  2.53 us

profile of v1, /device:TPU:1, one launch (start us, length us, event | category | flops | bytes accessed | tf_op | source)
XLA Modules:
  0.0 63.7 jit_solution(17586139425014305321)
XLA Ops:
  0.0 0.0 copy-start
  0.0 2.2 %copy.11.k1 = bf16[3,3,320,40]{3,2,1,0:T(8,128)(2,1)} copy(bf16[3,3,320,40]{2,3,1,0:T(8,128)(2,1)} %param.12) | data formatting | bytes 460800 | tf_op args[3]
  2.2 2.1 %copy.12.k2 = bf16[3,3,320,40]{3,2,1,0:T(8,128)(2,1)} copy(bf16[3,3,320,40]{2,3,1,0:T(8,128)(2,1)} %param.16) | data formatting | bytes 460800 | tf_op args[7]
  4.3 0.0 copy-done
  4.3 1.6 %copy.10.lat = bf16[1,8,256,320]{3,2,1,0:T(8,128)(2,1)} copy(bf16[1,8,256,320]{2,3,1,0:T(8,128)(2,1)S(1)} %copy-done) | data formatting | bytes 2621440 | tf_op args[0]
  5.9 55.3 %block.1 = bf16[1,8,256,320]{3,2,1,0:T(8,128)(2,1)} custom-call(bf16[1,8,256,320]{3,2,1,0:T(8,128)(2,1)} %copy.10.lat, f32[320]{0:T(512)} %g1.1, f32[320]{0:T(512)} %b1.1, bf16[3,3,320,40]{3,2,1,0:T(8,128)(2,1)} %copy.11.k1, f32[1,320]{1,0:T(1,128)} %ts.1, f32[320]{0:T(512)} %g2.1, f32[320]{0:T(512)} %b2.1, bf16[3,3,320,40]{3,2,1,0:T(8,128)(2,1)} %copy.12.k2, ...), custom_call_target="tpu_custom_call" | custom-call | tf_op jit(solution)/shard_map/block/pallas_call | solution.py:365
  61.2 2.5 %copy.13 = bf16[1,8,256,320]{2,3,1,0:T(8,128)(2,1)} copy(bf16[1,8,256,320]{3,2,1,0:T(8,128)(2,1)} %block.1) | data formatting | bytes 2621440 | tf_op jit(solution)/shard_map/block/pallas_call | solution.py:365
Async XLA Ops:
  0.0 4.3 %copy-start = (bf16[1,8,256,320]{2,3,1,0:T(8,128)(2,1)S(1)}, bf16[1,8,256,320]{2,3,1,0:T(8,128)(2,1)}, u32[]{:S(2)}) copy-start(bf16[1,8,256,320]{2,3,1,0:T(8,128)(2,1)} %param.9) | copy-start | bytes 3932164

commit v2 on v1

v2 whole, which is shorter than its diff:
```python
import functools

import jax
import jax.numpy as jnp
from jax import lax
from jax.experimental import pallas as pl
from jax.experimental.pallas import tpu as pltpu
from jax.sharding import PartitionSpec as P

MESH = pl.DeviceIdType.MESH
BF = jnp.bfloat16
F32 = jnp.float32
C = 320
MAIN = 256
LEFT = 64
TILES = 8
EPSILON = 1e-05
NZ = 8
NS = 32
ROWS = 8
COLS = 256
ORDER = (1, 7, 2, 6, 3, 5, 4)


def group_matrix():
    rows = lax.broadcasted_iota(jnp.int32, (384, 384), 0)
    cols = lax.broadcasted_iota(jnp.int32, (384, 384), 1)
    same = ((rows * 6554) >> 16) == ((cols * 6554) >> 16)
    return jnp.where(same, 1.0, 0.0).astype(BF)


def group_sum(vec, gmat):
    hi = vec.astype(BF)
    rest = vec - hi.astype(F32)
    mid = rest.astype(BF)
    low = (rest - mid.astype(F32)).astype(BF)
    lhs = jnp.concatenate([hi, mid, low, jnp.zeros((13, 384), BF)], axis=0)
    out = jnp.dot(lhs, gmat, preferred_element_type=F32)
    return out[0:1] + out[1:2] + out[2:3]


def to_lanes(block):
    return jnp.concatenate([block[0:1], block[1:2], block[2:3]], axis=1)


def to_rows(vec):
    return jnp.concatenate([vec[:, 0:128], vec[:, 128:256], vec[:, 256:384]], axis=0)


def combine(recv, gmat, gain, shift):
    means = recv[:, 0:3, :]
    squares = jnp.sum(recv[:, 3:6, :], axis=0)
    mean = group_sum(to_lanes(jnp.sum(means, axis=0)), gmat) * (1.0 / (NS * 10))
    centered = means - to_rows(mean)[None]
    total = squares + float(ROWS * COLS) * jnp.sum(centered * centered, axis=0)
    var = group_sum(to_lanes(total), gmat) * (1.0 / (10 * NS * ROWS * COLS))
    scale = 0.5 * lax.rsqrt(var + EPSILON)[:, :C] * gain
    offset = 0.5 * shift - mean[:, :C] * scale
    return columns(scale), columns(offset)


def columns(vec):
    return jnp.broadcast_to(vec, (128, C)).T


def wide(cols):
    return jnp.concatenate([cols, cols], axis=1)


def fold(v):
    return v[:, :128] + v[:, 128:]


def put_stats(st_ref, base, sums, squares):
    first = base.T[0:1]
    total = jnp.sum(sums.T, axis=0, keepdims=True)
    square = jnp.sum(squares.T, axis=0, keepdims=True)
    shift = total * (1.0 / (ROWS * COLS))
    st_ref[...] = jnp.zeros((8, 128), F32)
    for row, vec in ((0, first + shift), (3, square - total * shift)):
        st_ref[row : row + 1, :] = vec[:, 0:128]
        st_ref[row + 1 : row + 2, :] = vec[:, 128:256]
        st_ref[row + 2 : row + 3, 0:64] = vec[:, 256:320]


def act(v, scale, offset):
    half = v * wide(scale) + wide(offset)
    return (half + half * jnp.tanh(half)).astype(BF)


def taps(a):
    zero = jnp.zeros((a.shape[0], 1), BF)
    return jnp.concatenate([zero, a[:, : COLS - 1]], axis=1), a, jnp.concatenate([a[:, 1:], zero], axis=1)


def put_taps(a3, row, a):
    for i, t in enumerate(taps(a)):
        a3[row, i * MAIN : (i + 1) * MAIN] = t[:MAIN]
        a3[row, 3 * MAIN + i * LEFT : 3 * MAIN + (i + 1) * LEFT] = t[MAIN:]


def kernel(
    lat, g1, b1, k1, ts, g2, b2, k2, bias, out,
    x, a3, hid, kv, gath, w, gmat, par, st, recv, hs, hr, ob,
    lsem, osem, hsem, hrsem, ssem, srsem, wsem, wrsem,
):
    z = lax.axis_index("dp")
    s = lax.axis_index("space")
    y, xx, c = s // 8, (s // 2) % 4, s % 2
    part = c * 4 + (y % 2) * 2 + xx % 2

    barrier = pltpu.get_barrier_semaphore()
    for d in range(1, NS):
        pl.semaphore_signal(barrier, inc=1, device_id=(z, (s + d) % NS), device_id_type=MESH)
    for d in range(1, NZ):
        pl.semaphore_signal(barrier, inc=1, device_id=((z + d) % NZ, s), device_id_type=MESH)

    load_x = pltpu.make_async_copy(lat.at[0], x.at[pl.ds(1, ROWS)], lsem.at[0])
    load_k = [pltpu.make_async_copy(k, kv.at[i], lsem.at[1 + i]) for i, k in enumerate((k1, k2))]
    load_k[0].start()
    load_x.start()
    load_k[1].start()
    gmat[...] = group_matrix()
    for row in range(10):
        a3[row, 960:1024] = jnp.zeros((64, COLS), BF)
    par[0] = columns(ts[...])
    par[1] = columns(bias[...].reshape(1, C))

    def remote(src, dst, send, got, device):
        return pltpu.make_async_remote_copy(
            src_ref=src, dst_ref=dst, send_sem=send, recv_sem=got, device_id=device, device_id_type=MESH
        )

    def pack(n):
        for dy in range(3):
            pieces = [kv[n, dy, dx] for dx in range(3)]
            flat = jnp.concatenate(
                [t[:, :MAIN] for t in pieces] + [t[:, MAIN:] for t in pieces] + [jnp.zeros((40, LEFT), BF)],
                axis=1,
            )
            for p in range(TILES):
                gath[n, p, z, dy * 40 : dy * 40 + 40, :] = flat[:, p * 128 : (p + 1) * 128]
        for p in range(TILES):
            gath[n, p, z, 120:128, :] = jnp.zeros((8, 128), BF)

    def first(n, d):
        block = gath.at[n, part, z]
        return remote(block, block, wsem.at[n, d], wrsem.at[n, d], ((z + d) % NZ, s))

    def plane(y_step, x_step):
        return ((y + y_step) % 4 * 4 + (xx + x_step) % 4) * 2 + c

    def second(n, d):
        block = gath.at[n, part, (z - d) % NZ]
        sx = 1 if d % 2 == 0 else 3
        sy = 1 if (d // 2) % 2 == 0 else 3
        targets = (plane(0, sx), plane(sx, 0), plane(sy, sx))
        return [
            remote(block, block, wsem.at[n, 8 * (i + 1) + d], wrsem.at[n, 8 * (i + 1) + d], (z, t))
            for i, t in enumerate(targets)
        ]

    def third(n, d):
        block = gath.at[n, pl.ds(c * 4, 4), (z - d) % NZ]
        other = s + 1 - 2 * c
        return remote(block, block, wsem.at[n, 32 + d], wrsem.at[n, 32 + d], (z, other))

    def start_first(n):
        for d in ORDER:
            first(n, d).start()

    def go_second(n, d):
        first(n, d).wait_recv()
        for copy in second(n, d):
            copy.start()

    def go_third(n, d):
        for copy in second(n, d):
            copy.wait_recv()
        third(n, d).start()

    def end_gather(n):
        for d in ORDER:
            third(n, d).wait_recv()

    def drain(n):
        for d in ORDER:
            first(n, d).wait_send()
            for copy in second(n, d):
                copy.wait_send()
            third(n, d).wait_send()

    def arrange(n):
        for o in range(NZ):
            for dy in range(3):
                for p in range(TILES):
                    cols = slice(dy * 1024 + p * 128, dy * 1024 + p * 128 + 128)
                    w[n, o * 40 : o * 40 + 40, cols] = gath[n, p, o, dy * 40 : dy * 40 + 40, :]

    def stat_copy(n, d):
        return remote(st.at[n], recv.at[n, d - 1], ssem.at[n, d], srsem.at[n], (z, (s + d) % NS))

    def send_stats(n):
        for d in range(1, NS):
            stat_copy(n, d).start()
        recv[n, NS - 1] = st[n]

    def wait_stats(n):
        pltpu.make_async_copy(recv.at[n, pl.ds(0, NS - 1)], recv.at[n, pl.ds(0, NS - 1)], srsem.at[n]).wait()

    def conv(n, row):
        rhs = jnp.concatenate([a3[row + d] for d in range(3)], axis=0)
        return jnp.dot(w[n], rhs, preferred_element_type=F32)

    load_k[0].wait()
    pack(0)
    load_x.wait()
    base = jnp.broadcast_to(
        jnp.sum(fold(x[1].astype(F32)), axis=1, keepdims=True) * (1.0 / COLS), (C, 128)
    )
    par[2] = base

    def sum_row(i, carry):
        v = x[1 + i].astype(F32) - wide(par[2])
        par[3] += fold(v)
        par[4] += fold(v * v)
        return carry

    par[3] = jnp.zeros((C, 128), F32)
    par[4] = jnp.zeros((C, 128), F32)
    lax.fori_loop(0, ROWS, sum_row, 0)
    put_stats(st.at[0], par[2], par[3], par[4])

    pl.semaphore_wait(barrier, NS - 1 + NZ - 1)
    start_first(0)
    send_stats(0)
    halo = [
        remote(x.at[1], x.at[9], hsem.at[0], hrsem.at[0], (z, (s + NS - 1) % NS)),
        remote(x.at[8], x.at[0], hsem.at[1], hrsem.at[1], (z, (s + 1) % NS)),
    ]
    for copy in halo:
        copy.start()
    load_k[1].wait()
    pack(1)
    go_second(0, 1)
    go_second(0, 7)
    go_second(0, 2)
    go_second(0, 6)
    wait_stats(0)
    par[5], par[6] = combine(recv[0], gmat[...], g1[...].reshape(1, C), b1[...].reshape(1, C))

    def act_block(i, carry):
        low = pl.multiple_of(i * LEFT, LEFT)
        rows = pl.ds(low, LEFT)
        scale, offset = par[5, rows], par[6, rows]
        for row in range(1, 1 + ROWS):
            for k, t in enumerate(taps(act(x[row, rows].astype(F32), scale, offset))):
                at = jnp.where(i < 4, k * MAIN + low, 3 * MAIN + k * LEFT)
                a3[row, pl.ds(pl.multiple_of(at, LEFT), LEFT)] = t
        return carry

    lax.fori_loop(0, 5, act_block, 0)
    go_second(0, 3)
    go_second(0, 5)
    go_third(0, 1)
    go_third(0, 7)
    go_second(0, 4)
    start_first(1)
    go_third(0, 2)
    go_third(0, 6)

    for copy in halo:
        copy.wait_recv()
    for row, edge in ((0, 0), (9, NS - 1)):
        a = act(x[row].astype(F32), par[5], par[6])
        put_taps(a3, row, jnp.where(s == edge, jnp.zeros((C, COLS), BF), a))
    go_third(0, 3)
    go_third(0, 5)
    go_third(0, 4)
    end_gather(0)
    arrange(0)

    for row in range(ROWS):
        v = conv(0, row) + wide(par[0])
        hid[row] = v
        if row == 0:
            base = jnp.broadcast_to(jnp.sum(fold(v), axis=1, keepdims=True) * (1.0 / COLS), (C, 128))
            par[2] = base
            v = v - wide(base)
            par[3] = fold(v)
            par[4] = fold(v * v)
        else:
            v = v - wide(par[2])
            par[3] += fold(v)
            par[4] += fold(v * v)
        if row == 1:
            go_second(1, 1)
            go_second(1, 7)
        if row == 3:
            go_second(1, 2)
            go_second(1, 6)
        if row == 5:
            go_second(1, 3)
            go_second(1, 5)
            go_second(1, 4)
    put_stats(st.at[1], par[2], par[3], par[4])
    send_stats(1)
    for d in ORDER:
        go_third(1, d)
    end_gather(1)
    arrange(1)
    wait_stats(1)
    par[5], par[6] = combine(recv[1], gmat[...], g2[...].reshape(1, C), b2[...].reshape(1, C))

    sides = []
    for i, (row, step) in enumerate(((0, NS - 1), (ROWS - 1, 1))):
        a = act(hid[row], par[5], par[6])
        hs[i] = a
        copy = remote(hs.at[i], hr.at[1 - i], hsem.at[2 + i], hrsem.at[2 + i], (z, (s + step) % NS))
        copy.start()
        sides.append(copy)
        put_taps(a3, 1 + row, a)

    stores = []

    def finish(row):
        v = conv(1, row) + wide(par[1]) + x[1 + row].astype(F32)
        ob[row] = v.astype(BF)
        store = pltpu.make_async_copy(ob.at[row], out.at[0, row], osem.at[row])
        store.start()
        stores.append(store)

    put_taps(a3, 2, act(hid[1], par[5], par[6]))
    for row in range(1, ROWS - 1):
        if row < ROWS - 2:
            put_taps(a3, row + 2, act(hid[row + 1], par[5], par[6]))
        finish(row)
    for copy in sides:
        copy.wait_recv()
    zero = jnp.zeros((C, COLS), BF)
    put_taps(a3, 0, jnp.where(s == 0, zero, hr[0]))
    put_taps(a3, 9, jnp.where(s == NS - 1, zero, hr[1]))
    finish(0)
    finish(ROWS - 1)
    for n in range(2):
        for d in range(1, NS):
            stat_copy(n, d).wait_send()
        drain(n)
    for copy in halo + sides:
        copy.wait_send()
    for store in stores:
        store.wait()


def local(latents, gain_one, shift_one, kernel_one, time_shift, gain_two, shift_two, kernel_two, bias_two):
    hbm = pl.BlockSpec(memory_space=pl.ANY)
    vmem = pl.BlockSpec(memory_space=pltpu.VMEM)
    result = pl.pallas_call(
        kernel,
        out_shape=jax.ShapeDtypeStruct((1, ROWS, C, COLS), BF),
        in_specs=[hbm, vmem, vmem, hbm, vmem, vmem, vmem, hbm, vmem],
        out_specs=hbm,
        scratch_shapes=[
            pltpu.VMEM((10, C, COLS), BF),
            pltpu.VMEM((10, 1024, COLS), BF),
            pltpu.VMEM((ROWS, C, COLS), F32),
            pltpu.VMEM((2, 3, 3, 40, C), BF),
            pltpu.VMEM((2, TILES, NZ, 128, 128), BF),
            pltpu.VMEM((2, C, 3072), BF),
            pltpu.VMEM((384, 384), BF),
            pltpu.VMEM((7, C, 128), F32),
            pltpu.VMEM((2, 8, 128), F32),
            pltpu.VMEM((2, NS, 8, 128), F32),
            pltpu.VMEM((2, C, COLS), BF),
            pltpu.VMEM((2, C, COLS), BF),
            pltpu.VMEM((ROWS, C, COLS), BF),
            pltpu.SemaphoreType.DMA((3,)),
            pltpu.SemaphoreType.DMA((ROWS,)),
            pltpu.SemaphoreType.DMA((4,)),
            pltpu.SemaphoreType.DMA((4,)),
            pltpu.SemaphoreType.DMA((2, NS)),
            pltpu.SemaphoreType.DMA((2,)),
            pltpu.SemaphoreType.DMA((2, 40)),
            pltpu.SemaphoreType.DMA((2, 40)),
        ],
        compiler_params=pltpu.CompilerParams(
            collective_id=0, has_side_effects=True, vmem_limit_bytes=60 * 2**20
        ),
        name="block",
    )(
        latents.transpose(0, 1, 3, 2),
        gain_one,
        shift_one,
        kernel_one.transpose(0, 1, 3, 2),
        time_shift,
        gain_two,
        shift_two,
        kernel_two.transpose(0, 1, 3, 2),
        bias_two,
    )
    return result.transpose(0, 1, 3, 2)


def solution(mesh):
    return jax.shard_map(
        local,
        mesh=mesh,
        in_specs=(
            P("dp", "space", None, None),
            P(),
            P(),
            P(None, None, None, "dp"),
            P("dp", None),
            P(),
            P(),
            P(None, None, None, "dp"),
            P(),
        ),
        out_specs=P("dp", "space", None, None),
        check_vma=False,
    )
```

time: 63.9 us -> 49.9 us (0.78)
  Pallas kernels: 55.3 us -> 47.3 us
  local copies, waits for them, and re-layouts: 8.42 us -> 2.46 us
    pallas_call x1, Pallas kernels: 55.3 us -> 47.3 us  [local(): pl.pallas_call(kernel, out_shape=jax.ShapeDtypeStruct((1, ROWS, C, COLS),...]
    unnamed x5 -> x1, local copies, waits for them, and re-layouts: 5.88 us -> 2.46 us
    pallas_call x1 -> x0, local copies, waits for them, and re-layouts: 2.53 us -> none  [local(): pl.pallas_call(kernel, out_shape=jax.ShapeDtypeStruct((1, ROWS, COLS, C),...]
where the time goes in v2:
time: 49.9 us; the launch traced here: 49.8 us
  Pallas kernels  47.3 us (95%)
  local copies, waits for them, and re-layouts  2.46 us (5%)
    pallas_call x1, Pallas kernels, local(): pl.pallas_call(kernel, out_shape=jax.ShapeDtypeStruct((1, ROWS, C, COLS),...  47.3 us
    unnamed x1, local copies, waits for them, and re-layouts  2.46 us

profile of v2, /device:TPU:1, one launch (start us, length us, event | category | flops | bytes accessed | tf_op | source)
XLA Modules:
  0.0 49.8 jit_solution(6635139831274665319)
XLA Ops:
  0.0 47.3 %block.1 = bf16[1,8,320,256]{3,2,1,0:T(8,128)(2,1)} custom-call(bf16[1,8,320,256]{3,2,1,0:T(8,128)(2,1)} %bitcast.5, f32[320]{0:T(512)} %g1.1, f32[320]{0:T(512)} %b1.1, bf16[3,3,40,320]{3,2,1,0:T(8,128)(2,1)} %bitcast.6, f32[1,320]{1,0:T(1,128)} %ts.1, f32[320]{0:T(512)} %g2.1, f32[320]{0:T(512)} %b2.1, bf16[3,3,40,320]{3,2,1,0:T(8,128)(2,1)} %bitcast.7, ...), custom_call_target="tpu_custom_call" | custom-call | tf_op jit(solution)/shard_map/block/pallas_call | solution.py:358
  47.3 2.5 %copy.11 = bf16[1,8,256,320]{2,3,1,0:T(8,128)(2,1)} copy(bf16[1,8,256,320]{2,3,1,0:T(8,128)(2,1)} %bitcast.4) | data formatting | bytes 2621440

commit v3 on v2

--- a/solution.py
+++ b/solution.py
@@ -20,6 +20,13 @@
 ROWS = 8
 COLS = 256
 ORDER = (1, 7, 2, 6, 3, 5, 4)
+HOPS = (0, 1, 2, 1)
+PEERS = tuple(
+    sorted(
+        ((dy, dx, dc) for dy in range(4) for dx in range(4) for dc in range(2) if dy + dx + dc > 0),
+        key=lambda p: -10 * (HOPS[p[0]] + HOPS[p[1]]) - p[2],
+    )
+)
 
 
 def group_matrix():
@@ -101,8 +108,8 @@
 
 def kernel(
     lat, g1, b1, k1, ts, g2, b2, k2, bias, out,
-    x, a3, hid, kv, gath, w, gmat, par, st, recv, hs, hr, ob,
-    lsem, osem, hsem, hrsem, ssem, srsem, wsem, wrsem,
+    x, a3, hid, kv, gath, w, gmat, par, st, recv, hs, hr,
+    lsem, hsem, hrsem, ssem, srsem, wsem, wrsem,
 ):
     z = lax.axis_index("dp")
     s = lax.axis_index("space")
@@ -174,10 +181,11 @@
         for copy in second(n, d):
             copy.start()
 
-    def go_third(n, d):
-        for copy in second(n, d):
-            copy.wait_recv()
-        third(n, d).start()
+    def go_third(n):
+        for d in ORDER:
+            for copy in second(n, d):
+                copy.wait_recv()
+            third(n, d).start()
 
     def end_gather(n):
         for d in ORDER:
@@ -190,15 +198,20 @@
                 copy.wait_send()
             third(n, d).wait_send()
 
-    def arrange(n):
-        for o in range(NZ):
-            for dy in range(3):
-                for p in range(TILES):
-                    cols = slice(dy * 1024 + p * 128, dy * 1024 + p * 128 + 128)
-                    w[n, o * 40 : o * 40 + 40, cols] = gath[n, p, o, dy * 40 : dy * 40 + 40, :]
+    def arrange(n, half):
+        def tile(q, carry):
+            for o in range(NZ):
+                for dy in range(3):
+                    cols = pl.ds(pl.multiple_of(dy * 512 + q * 128, 128), 128)
+                    w[n, half, o * 40 : o * 40 + 40, cols] = gath[n, half * 4 + q, o, dy * 40 : dy * 40 + 40, :]
+            return carry
+
+        lax.fori_loop(0, 4, tile, 0)
 
     def stat_copy(n, d):
-        return remote(st.at[n], recv.at[n, d - 1], ssem.at[n, d], srsem.at[n], (z, (s + d) % NS))
+        dy, dx, dc = PEERS[d - 1]
+        peer = ((y + dy) % 4 * 4 + (xx + dx) % 4) * 2 + (c + dc) % 2
+        return remote(st.at[n], recv.at[n, d - 1], ssem.at[n, d], srsem.at[n], (z, peer))
 
     def send_stats(n):
         for d in range(1, NS):
@@ -208,9 +221,14 @@
     def wait_stats(n):
         pltpu.make_async_copy(recv.at[n, pl.ds(0, NS - 1)], recv.at[n, pl.ds(0, NS - 1)], srsem.at[n]).wait()
 
-    def conv(n, row):
-        rhs = jnp.concatenate([a3[row + d] for d in range(3)], axis=0)
-        return jnp.dot(w[n], rhs, preferred_element_type=F32)
+    def conv_half(row, half):
+        rows = pl.ds(pl.multiple_of(half * 512, 512), 512)
+        rhs = jnp.concatenate([a3[row + d, rows] for d in range(3)], axis=0)
+        return jnp.dot(w[0, half], rhs, preferred_element_type=F32)
+
+    def conv_two(row):
+        rhs = jnp.concatenate([a3[row + d, h * 512 : h * 512 + 512] for h in range(2) for d in range(3)], axis=0)
+        return jnp.dot(jnp.concatenate([w[1, 0], w[1, 1]], axis=1), rhs, preferred_element_type=F32)
 
     load_k[0].wait()
     pack(0)
@@ -262,26 +280,24 @@
     lax.fori_loop(0, 5, act_block, 0)
     go_second(0, 3)
     go_second(0, 5)
-    go_third(0, 1)
-    go_third(0, 7)
     go_second(0, 4)
     start_first(1)
-    go_third(0, 2)
-    go_third(0, 6)
-
     for copy in halo:
         copy.wait_recv()
     for row, edge in ((0, 0), (9, NS - 1)):
         a = act(x[row].astype(F32), par[5], par[6])
         put_taps(a3, row, jnp.where(s == edge, jnp.zeros((C, COLS), BF), a))
-    go_third(0, 3)
-    go_third(0, 5)
-    go_third(0, 4)
+    go_third(0)
+    arrange(0, c)
+    for row in range(ROWS):
+        hid[row] = conv_half(row, c)
+        if row == 5:
+            go_second(1, 1)
+            go_second(1, 7)
     end_gather(0)
-    arrange(0)
-
+    arrange(0, 1 - c)
     for row in range(ROWS):
-        v = conv(0, row) + wide(par[0])
+        v = hid[row] + conv_half(row, 1 - c) + wide(par[0])
         hid[row] = v
         if row == 0:
             base = jnp.broadcast_to(jnp.sum(fold(v), axis=1, keepdims=True) * (1.0 / COLS), (C, 128))
@@ -294,21 +310,17 @@
             par[3] += fold(v)
             par[4] += fold(v * v)
         if row == 1:
-            go_second(1, 1)
-            go_second(1, 7)
-        if row == 3:
             go_second(1, 2)
             go_second(1, 6)
-        if row == 5:
+        if row == 4:
             go_second(1, 3)
             go_second(1, 5)
+        if row == 6:
             go_second(1, 4)
     put_stats(st.at[1], par[2], par[3], par[4])
     send_stats(1)
-    for d in ORDER:
-        go_third(1, d)
-    end_gather(1)
-    arrange(1)
+    go_third(1)
+    arrange(1, c)
     wait_stats(1)
     par[5], par[6] = combine(recv[1], gmat[...], g2[...].reshape(1, C), b2[...].reshape(1, C))
 
@@ -320,15 +332,12 @@
         copy.start()
         sides.append(copy)
         put_taps(a3, 1 + row, a)
-
-    stores = []
+    end_gather(1)
+    arrange(1, 1 - c)
 
     def finish(row):
-        v = conv(1, row) + wide(par[1]) + x[1 + row].astype(F32)
-        ob[row] = v.astype(BF)
-        store = pltpu.make_async_copy(ob.at[row], out.at[0, row], osem.at[row])
-        store.start()
-        stores.append(store)
+        v = conv_two(row) + wide(par[1]) + x[1 + row].astype(F32)
+        out[0, row] = v.astype(BF)
 
     put_taps(a3, 2, act(hid[1], par[5], par[6]))
     for row in range(1, ROWS - 1):
@@ -348,8 +357,6 @@
         drain(n)
     for copy in halo + sides:
         copy.wait_send()
-    for store in stores:
-        store.wait()
 
 
 def local(latents, gain_one, shift_one, kernel_one, time_shift, gain_two, shift_two, kernel_two, bias_two):
@@ -357,25 +364,23 @@
     vmem = pl.BlockSpec(memory_space=pltpu.VMEM)
     result = pl.pallas_call(
         kernel,
-        out_shape=jax.ShapeDtypeStruct((1, ROWS, C, COLS), BF),
+        out_shape=pltpu.VMEM((1, ROWS, C, COLS), BF),
         in_specs=[hbm, vmem, vmem, hbm, vmem, vmem, vmem, hbm, vmem],
-        out_specs=hbm,
+        out_specs=vmem,
         scratch_shapes=[
             pltpu.VMEM((10, C, COLS), BF),
             pltpu.VMEM((10, 1024, COLS), BF),
             pltpu.VMEM((ROWS, C, COLS), F32),
             pltpu.VMEM((2, 3, 3, 40, C), BF),
             pltpu.VMEM((2, TILES, NZ, 128, 128), BF),
-            pltpu.VMEM((2, C, 3072), BF),
+            pltpu.VMEM((2, 2, C, 1536), BF),
             pltpu.VMEM((384, 384), BF),
             pltpu.VMEM((7, C, 128), F32),
             pltpu.VMEM((2, 8, 128), F32),
             pltpu.VMEM((2, NS, 8, 128), F32),
             pltpu.VMEM((2, C, COLS), BF),
             pltpu.VMEM((2, C, COLS), BF),
-            pltpu.VMEM((ROWS, C, COLS), BF),
             pltpu.SemaphoreType.DMA((3,)),
-            pltpu.SemaphoreType.DMA((ROWS,)),
             pltpu.SemaphoreType.DMA((4,)),
             pltpu.SemaphoreType.DMA((4,)),
             pltpu.SemaphoreType.DMA((2, NS)),

time: 49.9 us -> 45.5 us (0.912)
  Pallas kernels: 47.3 us -> 44.1 us
  local copies, waits for them, and re-layouts: 2.46 us -> 1.06 us
    pallas_call x1, Pallas kernels: 47.3 us -> 44.1 us  [local(): pl.pallas_call(kernel, out_shape=pltpu.VMEM((1, ROWS, C, COLS), BF), in_s...]
    unnamed x1, local copies, waits for them, and re-layouts: 2.46 us -> 1.06 us
where the time goes in v3:
time: 45.5 us; the launch traced here: 45.2 us
  Pallas kernels  44.1 us (97%)
  local copies, waits for them, and re-layouts  1.06 us (2%)
    pallas_call x1, Pallas kernels, local(): pl.pallas_call(kernel, out_shape=pltpu.VMEM((1, ROWS, C, COLS), BF), in_s...  44.1 us
    unnamed x1, local copies, waits for them, and re-layouts  1.06 us

profile of v3, /device:TPU:1, one launch (start us, length us, event | category | flops | bytes accessed | tf_op | source)
XLA Modules:
  0.0 45.2 jit_solution(11695117301760276876)
XLA Ops:
  0.0 44.1 %block.1 = bf16[1,8,320,256]{3,2,1,0:T(8,128)(2,1)S(1)} custom-call(bf16[1,8,320,256]{3,2,1,0:T(8,128)(2,1)} %bitcast.5, f32[320]{0:T(512)} %g1.1, f32[320]{0:T(512)} %b1.1, bf16[3,3,40,320]{3,2,1,0:T(8,128)(2,1)} %bitcast.6, f32[1,320]{1,0:T(1,128)} %ts.1, f32[320]{0:T(512)} %g2.1, f32[320]{0:T(512)} %b2.1, bf16[3,3,40,320]{3,2,1,0:T(8,128)(2,1)} %bitcast.7, ...), custom_call_target="tpu_custom_call" | custom-call | tf_op jit(solution)/shard_map/block/pallas_call | solution.py:365
  44.1 1.1 %copy.11 = bf16[1,8,256,320]{2,3,1,0:T(8,128)(2,1)} copy(bf16[1,8,256,320]{2,3,1,0:T(8,128)(2,1)S(1)} %bitcast.4) | data formatting | bytes 2621440

commit v4 on v3

--- a/solution.py
+++ b/solution.py
@@ -321,6 +321,11 @@
     send_stats(1)
     go_third(1)
     arrange(1, c)
+    for d in range(1, NS):
+        stat_copy(0, d).wait_send()
+    drain(0)
+    for copy in halo:
+        copy.wait_send()
     wait_stats(1)
     par[5], par[6] = combine(recv[1], gmat[...], g2[...].reshape(1, C), b2[...].reshape(1, C))
 
@@ -344,6 +349,9 @@
         if row < ROWS - 2:
             put_taps(a3, row + 2, act(hid[row + 1], par[5], par[6]))
         finish(row)
+    for d in range(1, NS):
+        stat_copy(1, d).wait_send()
+    drain(1)
     for copy in sides:
         copy.wait_recv()
     zero = jnp.zeros((C, COLS), BF)
@@ -351,11 +359,7 @@
     put_taps(a3, 9, jnp.where(s == NS - 1, zero, hr[1]))
     finish(0)
     finish(ROWS - 1)
-    for n in range(2):
-        for d in range(1, NS):
-            stat_copy(n, d).wait_send()
-        drain(n)
-    for copy in halo + sides:
+    for copy in sides:
         copy.wait_send()
 
 

time: 45.5 us -> 45.3 us (level)
  no operation moved by 1% of the time
where the time goes in v4:
time: 45.3 us; the launch traced here: 45.1 us
  Pallas kernels  44 us (97%)
  local copies, waits for them, and re-layouts  1.06 us (2%)
    pallas_call x1, Pallas kernels, local(): pl.pallas_call(kernel, out_shape=pltpu.VMEM((1, ROWS, C, COLS), BF), in_s...  44 us
    unnamed x1, local copies, waits for them, and re-layouts  1.06 us

profile of v4, /device:TPU:1, one launch (start us, length us, event | category | flops | bytes accessed | tf_op | source)
XLA Modules:
  0.0 45.1 jit_solution(13234820688681074688)
XLA Ops:
  0.0 44.0 %block.1 = bf16[1,8,320,256]{3,2,1,0:T(8,128)(2,1)S(1)} custom-call(bf16[1,8,320,256]{3,2,1,0:T(8,128)(2,1)} %bitcast.5, f32[320]{0:T(512)} %g1.1, f32[320]{0:T(512)} %b1.1, bf16[3,3,40,320]{3,2,1,0:T(8,128)(2,1)} %bitcast.6, f32[1,320]{1,0:T(1,128)} %ts.1, f32[320]{0:T(512)} %g2.1, f32[320]{0:T(512)} %b2.1, bf16[3,3,40,320]{3,2,1,0:T(8,128)(2,1)} %bitcast.7, ...), custom_call_target="tpu_custom_call" | custom-call | tf_op jit(solution)/shard_map/block/pallas_call | solution.py:369
  44.0 1.1 %copy.11 = bf16[1,8,256,320]{2,3,1,0:T(8,128)(2,1)} copy(bf16[1,8,256,320]{2,3,1,0:T(8,128)(2,1)S(1)} %bitcast.4) | data formatting | bytes 2621440

commit v5 on v4

--- a/solution.py
+++ b/solution.py
@@ -336,7 +336,8 @@
         copy = remote(hs.at[i], hr.at[1 - i], hsem.at[2 + i], hrsem.at[2 + i], (z, (s + step) % NS))
         copy.start()
         sides.append(copy)
-        put_taps(a3, 1 + row, a)
+    for i, row in enumerate((0, ROWS - 1)):
+        put_taps(a3, 1 + row, hs[i])
     end_gather(1)
     arrange(1, 1 - c)
 

time: 45.3 us -> 45.3 us (level)
  no operation moved by 1% of the time
where the time goes in v5:
time: 45.3 us; the launch traced here: 45.2 us
  Pallas kernels  44.1 us (97%)
  local copies, waits for them, and re-layouts  1.06 us (2%)
    pallas_call x1, Pallas kernels, local(): pl.pallas_call(kernel, out_shape=pltpu.VMEM((1, ROWS, C, COLS), BF), in_s...  44.1 us
    unnamed x1, local copies, waits for them, and re-layouts  1.06 us

profile of v5, /device:TPU:1, one launch (start us, length us, event | category | flops | bytes accessed | tf_op | source)
XLA Modules:
  0.0 45.2 jit_solution(14970271261767275886)
XLA Ops:
  0.0 44.1 %block.1 = bf16[1,8,320,256]{3,2,1,0:T(8,128)(2,1)S(1)} custom-call(bf16[1,8,320,256]{3,2,1,0:T(8,128)(2,1)} %bitcast.5, f32[320]{0:T(512)} %g1.1, f32[320]{0:T(512)} %b1.1, bf16[3,3,40,320]{3,2,1,0:T(8,128)(2,1)} %bitcast.6, f32[1,320]{1,0:T(1,128)} %ts.1, f32[320]{0:T(512)} %g2.1, f32[320]{0:T(512)} %b2.1, bf16[3,3,40,320]{3,2,1,0:T(8,128)(2,1)} %bitcast.7, ...), custom_call_target="tpu_custom_call" | custom-call | tf_op jit(solution)/shard_map/block/pallas_call | solution.py:370
  44.1 1.1 %copy.11 = bf16[1,8,256,320]{2,3,1,0:T(8,128)(2,1)} copy(bf16[1,8,256,320]{2,3,1,0:T(8,128)(2,1)S(1)} %bitcast.4) | data formatting | bytes 2621440
